TPU v7x, 256 devices: a whole 4x4x8 slice. The times are simulated.
256 devices in a mesh: ctx: 32 (over y_hi, z, core), kvh: 8 (over y_lo, x).
Axes of the slice: x: 4, y: 4 (y_hi: 2, y_lo: 2; y = y_hi * 2 + y_lo), z: 8, core: 2. Of those that a mesh axis runs over, the one named last changes fastest.
Arguments:
- q_proj: bfloat16 [16384, 8192], P('ctx', 'kvh'), may hold values from -10 to 10
- key_projection: bfloat16 [16384, 1024], P('ctx', 'kvh'), may hold values from -10 to 10
- value_projection: bfloat16 [16384, 1024], P('ctx', 'kvh'), may hold values from -6 to 6
- doc_ids: int32 [16384], P(('ctx', 'kvh')), may hold values from 0 to 15, never falling along the last dimension, each value on 1 to 2048 neighbouring positions
Outputs:
- attended: bfloat16 [16384, 8192], P('ctx', 'kvh')
Inputs may be any that keep to these rules, and one draw needn't show every extreme that they name: `doc_ids`: ids never fall along the sequence; every answer has 1 to 2048 tokens, one exactly that many.
All inputs are finite; a program needn't handle non-finite values.
Results may differ from a plain program's by a relative error of at most 0.011.
Values may be sent and summed in bfloat16 or wider, within the bound.
No kernel may reach another device: no remote copies, remote signals or barrier semaphores. Data moves between devices by JAX's collectives and lax.ppermute only.
A program may use at most 64 MiB of HBM per device.

v0:
```python
import jax
import jax.numpy as jnp
from jax import lax
from jax.sharding import PartitionSpec as P

HEAD_SIZE = 128
GROUP = 8


NEG = -1e30
THETA = 1000000.0


def shifted(value, axis, steps):
    count = lax.axis_size(axis)
    leading, last = (max(0, -steps), min(count, count - steps))
    return lax.ppermute(value, axis, [(source, source + steps) for source in range(leading, last)])


def apply_rotary(x, token_positions):
    half = HEAD_SIZE // 2
    inv = THETA ** (-(2.0 * jnp.arange(half, dtype=jnp.float32)) / HEAD_SIZE)
    angle = token_positions.astype(jnp.float32)[:, None] * inv[None, :]
    cosine = jnp.cos(angle)[:, None, :]
    sine = jnp.sin(angle)[:, None, :]
    first = x[..., :half].astype(jnp.float32)
    second = x[..., half:].astype(jnp.float32)
    rotated = jnp.concatenate(
        [first * cosine - second * sine, second * cosine + first * sine], axis=-1
    )
    return rotated.astype(jnp.bfloat16)


def local(q_proj, key_projection, value_projection, doc_ids):
    tok_count = key_projection.shape[0]
    kv_heads = key_projection.shape[1] // HEAD_SIZE
    window = 4 * tok_count
    scale = 1.0 / jnp.sqrt(jnp.float32(HEAD_SIZE))
    local_ids = lax.all_gather(doc_ids, "kvh", axis=0, tiled=True)
    ids_float = local_ids.astype(jnp.bfloat16)
    token_positions = lax.axis_index("ctx") * tok_count + jnp.arange(tok_count, dtype=jnp.int32)
    queries = apply_rotary(q_proj.reshape(tok_count, kv_heads * GROUP, HEAD_SIZE), token_positions)
    key_rows = apply_rotary(key_projection.reshape(tok_count, kv_heads, HEAD_SIZE), token_positions)
    value_rows = value_projection.reshape(tok_count, kv_heads, HEAD_SIZE)
    qrows = queries.reshape(tok_count, kv_heads, GROUP, HEAD_SIZE).transpose(1, 2, 0, 3)
    state = (
        jnp.full((kv_heads, GROUP, tok_count), NEG, jnp.float32),
        jnp.zeros((kv_heads, GROUP, tok_count), jnp.float32),
        jnp.zeros((kv_heads, GROUP, tok_count, HEAD_SIZE), jnp.float32),
    )

    def absorb(carry, key_block, value_block, key_ids, key_pos):
        visible = (ids_float[:, None] == key_ids[None, :]) & (
            token_positions[:, None] >= key_pos[None, :]
        )
        visible = (
            visible
            & (token_positions[:, None] - key_pos[None, :] < window)
            & (key_pos[None, :] >= 0)
        )
        key_heads = key_block.transpose(1, 0, 2)
        value_heads = value_block.transpose(1, 0, 2)

        def one_head(item):
            running, total, acc, qgroup, kgroup, vgroup = item
            scores = (
                jnp.einsum("htd,sd->hts", qgroup, kgroup, preferred_element_type=jnp.float32)
                * scale
            )
            scores = jnp.where(visible[None, :, :], scores, NEG)
            newmax = jnp.maximum(running, jnp.max(scores, axis=-1))
            factor = jnp.exp(running - newmax)
            weights = jnp.exp(scores - newmax[:, :, None])
            total = total * factor + jnp.sum(weights, axis=-1)
            rounded = weights.astype(jnp.bfloat16)
            update = jnp.einsum("hts,sd->htd", rounded, vgroup, preferred_element_type=jnp.float32)
            return (newmax, total, acc * factor[:, :, None] + update)

        return lax.map(one_head, (carry[0], carry[1], carry[2], qrows, key_heads, value_heads))

    state = absorb(state, key_rows, value_rows, ids_float, token_positions)
    outgoing = (key_rows, value_rows, ids_float)
    arrived = outgoing
    for step in range(1, 5):
        arrived = shifted((arrived[0], arrived[1], arrived[2]), "ctx", 1)
        state = absorb(
            state, arrived[0], arrived[1], arrived[2], token_positions - step * tok_count
        )
    running, total, acc = state
    result = acc / total[:, :, :, None]
    result = result.transpose(2, 0, 1, 3).reshape(tok_count, kv_heads * GROUP * HEAD_SIZE)
    return result.astype(jnp.bfloat16)


def solution(mesh):
    in_specs = (P("ctx", "kvh"), P("ctx", "kvh"), P("ctx", "kvh"), P(("ctx", "kvh")))
    out_specs = P("ctx", "kvh")
    return jax.shard_map(local, mesh=mesh, in_specs=in_specs, out_specs=out_specs, check_vma=False)
```

profile of v0, /device:TPU:16, one launch (start us, length us, event | category | flops | bytes accessed | tf_op | source)
XLA Modules:
  0.0 127.3 jit_solution(17503346513081041514)
XLA Ops:
  0.0 1.3 dynamic-slice.14
  1.9 0.9 dynamic-update-slice
  2.8 11.7 %all-reduce = s32[512]{0:T(512)S(1)} all-reduce(s32[512]{0:T(512)S(1)} %dynamic-update-slice), channel_id=1, replica_groups=mesh['ctx'=32,'kvh'=8] {'kvh'}, use_global_device_ids=true, to_apply=%add | all-reduce | flops 512 | bytes 4096
  14.5 1.9 %collective-permute-start = (bf16[512]{0:T(512)(128)(2,1)S(1)}, bf16[512]{0:T(512)(128)(2,1)}, u32[]{:S(2)}, u32[]{:S(2)}) collective-permute-start(bf16[512]{0:T(512)(128)(2,1)S(1)} %convert_element_type.73), channel_id=1, source_target_pairs={{0,8},{8,16},{16,24},{24,32},{32,40},{40,48},{48,56},{56,64},{64,7... | collective-permute-start | bytes 3080 | tf_op jit(solution)/shard_map/ppermute | solution.py:17
  16.5 2.1 %fusion.51 = (bf16[512,1,64]{2,0,1:T(8,128)(2,1)S(1)}, bf16[512,1,64]{2,0,1:T(8,128)(2,1)S(1)}) fusion(f32[64]{0:T(128)S(1)} %multiply_power_fusion, f32[512]{0:T(512)S(1)} %fusion.78, bf16[512,1,128]{2,0,1:T(8,128)(2,1)} %bitcast.82), kind=kLoop, calls=%fused_computation.71 | loop fusion | flops 360448 | bytes 264448 | tf_op jit(solution)/shard_map/convert.5
  18.6 0.8 pad_maximum_fusion
  19.4 3.9 %collective-permute-start.1 = (bf16[512,1,128]{2,0,1:T(8,128)(2,1)}, bf16[512,1,128]{2,0,1:T(8,128)(2,1)S(1)}, u32[]{:S(2)}, u32[]{:S(2)}) collective-permute-start(bf16[512,1,128]{2,0,1:T(8,128)(2,1)} %pad_maximum_fusion), channel_id=1, source_target_pairs={{0,8},{8,16},{16,24},{24,32},{32,40},{40,48},{48,56},{56,64},{64,7... | collective-permute-start | bytes 393224 | tf_op jit(solution)/shard_map/ppermute | solution.py:17
  23.3 1.7 %copy.18 = bf16[512,128]{0,1:T(8,128)(2,1)} copy(bf16[512,128]{1,0:T(8,128)(2,1)} %param.6) | data formatting | bytes 262144 | tf_op args[2]
  25.0 1.9 %collective-permute-start.2 = (bf16[512,1,128]{0,2,1:T(8,128)(2,1)}, bf16[512,1,128]{0,2,1:T(8,128)(2,1)}, u32[]{:S(2)}, u32[]{:S(2)}) collective-permute-start(bf16[512,1,128]{0,2,1:T(8,128)(2,1)} %bitcast.14), channel_id=1, source_target_pairs={{0,8},{8,16},{16,24},{24,32},{32,40},{40,48},{48,56},{56,64},{64,7... | collective-permute-start | bytes 393224 | tf_op jit(solution)/shard_map/ppermute | solution.py:17
  26.9 0.6 fusion.75
  27.5 1.0 multiply_cosine_fusion.1
  28.5 1.5 %copy.13 = bf16[512,1024]{0,1:T(8,128)(2,1)S(1)} copy(bf16[512,1024]{1,0:T(8,128)(2,1)} %param.4) | data formatting | bytes 2097152 | tf_op args[0]
  30.1 0.5 copy.31
  30.6 0.5 copy.32
  31.1 0.7 fusion.35
  31.8 0.6 maximum_bitcast_fusion
  32.4 3.9 %collective-permute-start.3 = (bf16[512]{0:T(512)(128)(2,1)}, bf16[512]{0:T(512)(128)(2,1)S(1)}, u32[]{:S(2)}, u32[]{:S(2)}) collective-permute-start(bf16[512]{0:T(512)(128)(2,1)} %collective-permute-done), channel_id=1, source_target_pairs={{0,8},{8,16},{16,24},{24,32},{32,40},{40,48},{48,56},{56,64},{64,7... | collective-permute-start | bytes 3080 | tf_op jit(solution)/shard_map/ppermute | solution.py:17
  36.3 4.8 %collective-permute-done.3 = bf16[512]{0:T(512)(128)(2,1)S(1)} collective-permute-done((bf16[512]{0:T(512)(128)(2,1)}, bf16[512]{0:T(512)(128)(2,1)S(1)}, u32[]{:S(2)}, u32[]{:S(2)}) %collective-permute-start.3) | collective-permute-done | bytes 1056 | tf_op jit(solution)/shard_map/ppermute | solution.py:17
  41.1 1.9 %collective-permute-start.6 = (bf16[512]{0:T(512)(128)(2,1)S(1)}, bf16[512]{0:T(512)(128)(2,1)S(1)}, u32[]{:S(2)}, u32[]{:S(2)}) collective-permute-start(bf16[512]{0:T(512)(128)(2,1)S(1)} %collective-permute-done.3), channel_id=1, source_target_pairs={{0,8},{8,16},{16,24},{24,32},{32,40},{40,48},{48,56},{56,64},{64,7... | collective-permute-start | bytes 3080 | tf_op jit(solution)/shard_map/ppermute | solution.py:17
  43.0 6.6 %collective-permute-done.6 = bf16[512]{0:T(512)(128)(2,1)S(1)} collective-permute-done((bf16[512]{0:T(512)(128)(2,1)S(1)}, bf16[512]{0:T(512)(128)(2,1)S(1)}, u32[]{:S(2)}, u32[]{:S(2)}) %collective-permute-start.6) | collective-permute-done | bytes 1056 | tf_op jit(solution)/shard_map/ppermute | solution.py:17
  49.6 1.9 %collective-permute-start.9 = (bf16[512]{0:T(512)(128)(2,1)S(1)}, bf16[512]{0:T(512)(128)(2,1)S(1)}, u32[]{:S(2)}, u32[]{:S(2)}) collective-permute-start(bf16[512]{0:T(512)(128)(2,1)S(1)} %collective-permute-done.6), channel_id=1, source_target_pairs={{0,8},{8,16},{16,24},{24,32},{32,40},{40,48},{48,56},{56,64},{64,7... | collective-permute-start | bytes 3080 | tf_op jit(solution)/shard_map/ppermute | solution.py:17
  51.5 6.6 %collective-permute-done.9 = bf16[512]{0:T(512)(128)(2,1)S(1)} collective-permute-done((bf16[512]{0:T(512)(128)(2,1)S(1)}, bf16[512]{0:T(512)(128)(2,1)S(1)}, u32[]{:S(2)}, u32[]{:S(2)}) %collective-permute-start.9) | collective-permute-done | bytes 1056 | tf_op jit(solution)/shard_map/ppermute | solution.py:17
  58.1 2.9 %fusion.37 = (pred[512,512]{0,1:T(8,128)(4,1)S(1)}, pred[512,512]{0,1:T(8,128)(4,1)S(1)}, pred[512,512]{0,1:T(8,128)(4,1)S(1)}, pred[512,512]{0,1:T(8,128)(4,1)S(1)}, pred[512,512]{0,1:T(8,128)(4,1)S(1)}) fusion(s32[512]{0:T(512)S(1)} %get-tuple-element.170, pred[512]{0:T(512)(128)(4,1)S(1)} %get-tuple-element.184, ...), kind=kLoop, calls=%fused_computation.53 | loop fusion | flops 10747904 | bytes 1328640 | tf_op jit(solution)/shard_map/and | solution.py:57
  61.0 1.6 %fusion = (f32[8,512]{1,0:T(8,128)S(1)}, f32[8,512,512]{1,2,0:T(8,128)S(1)}) fusion(pred[512,512]{0,1:T(8,128)(4,1)S(1)} %get-tuple-element.142, bf16[8,512,128]{2,1,0:T(8,128)(2,1)S(1)} %maximum_bitcast_fusion, bf16[512,64]{1,0:T(8,128)(2,1)S(1)} %bitcast.80, bf16[512,64]{1,0:T(8,128)(2,1)S(1)} %bitcast.79), kind=kOutput, calls=%fused_computation.10 | convolution fusion | flops 543420416 | bytes 9846784 | tf_op jit(solution)/shard_map/while/body/eval_jaxpr/htd,sd->hts/dot_general | solution.py:67
  62.6 1.9 %collective-permute-start.4 = (bf16[512,1,128]{2,0,1:T(8,128)(2,1)S(1)}, bf16[512,1,128]{2,0,1:T(8,128)(2,1)S(1)}, u32[]{:S(2)}, u32[]{:S(2)}) collective-permute-start(bf16[512,1,128]{2,0,1:T(8,128)(2,1)S(1)} %collective-permute-done.1), channel_id=1, source_target_pairs={{0,8},{8,16},{16,24},{24,32},{32,40},{40,48},{48,56},{56,64},{64,7... | collective-permute-start | bytes 393224 | tf_op jit(solution)/shard_map/ppermute | solution.py:17
  64.5 1.6 %fusion.1 = (f32[8,512]{1,0:T(8,128)S(1)}, f32[8,512,512]{1,2,0:T(8,128)S(1)}) fusion(pred[512,512]{0,1:T(8,128)(4,1)S(1)} %get-tuple-element.144, bf16[8,512,128]{2,1,0:T(8,128)(2,1)S(1)} %maximum_bitcast_fusion, bf16[512,1,128]{2,0,1:T(8,128)(2,1)S(1)} %collective-permute-done.1), kind=kOutput, calls=%fused_computation.11 | convolution fusion | flops 543158272 | bytes 9846784 | tf_op jit(solution)/shard_map/while/body/eval_jaxpr/htd,sd->hts/dot_general | solution.py:67
  66.1 1.9 %collective-permute-start.5 = (bf16[512,1,128]{0,2,1:T(8,128)(2,1)}, bf16[512,1,128]{0,2,1:T(8,128)(2,1)S(1)}, u32[]{:S(2)}, u32[]{:S(2)}) collective-permute-start(bf16[512,1,128]{0,2,1:T(8,128)(2,1)} %collective-permute-done.2), channel_id=1, source_target_pairs={{0,8},{8,16},{16,24},{24,32},{32,40},{40,48},{48,56},{56,64},{64,7... | collective-permute-start | bytes 393224 | tf_op jit(solution)/shard_map/ppermute | solution.py:17
  68.0 4.5 %collective-permute-done.4 = bf16[512,1,128]{2,0,1:T(8,128)(2,1)S(1)} collective-permute-done((bf16[512,1,128]{2,0,1:T(8,128)(2,1)S(1)}, bf16[512,1,128]{2,0,1:T(8,128)(2,1)S(1)}, u32[]{:S(2)}, u32[]{:S(2)}) %collective-permute-start.4) | collective-permute-done | bytes 131104 | tf_op jit(solution)/shard_map/ppermute | solution.py:17
  72.5 1.9 %collective-permute-start.7 = (bf16[512,1,128]{2,0,1:T(8,128)(2,1)S(1)}, bf16[512,1,128]{2,0,1:T(8,128)(2,1)S(1)}, u32[]{:S(2)}, u32[]{:S(2)}) collective-permute-start(bf16[512,1,128]{2,0,1:T(8,128)(2,1)S(1)} %collective-permute-done.4), channel_id=1, source_target_pairs={{0,8},{8,16},{16,24},{24,32},{32,40},{40,48},{48,56},{56,64},{64,7... | collective-permute-start | bytes 393224 | tf_op jit(solution)/shard_map/ppermute | solution.py:17
  74.4 1.6 %fusion.2 = (f32[8,512]{1,0:T(8,128)S(1)}, f32[8,512,512]{1,2,0:T(8,128)S(1)}) fusion(pred[512,512]{0,1:T(8,128)(4,1)S(1)} %get-tuple-element.146, bf16[8,512,128]{2,1,0:T(8,128)(2,1)S(1)} %maximum_bitcast_fusion, bf16[512,1,128]{2,0,1:T(8,128)(2,1)S(1)} %collective-permute-done.4), kind=kOutput, calls=%fused_computation.12 | convolution fusion | flops 543158272 | bytes 9846784 | tf_op jit(solution)/shard_map/while/body/eval_jaxpr/htd,sd->hts/dot_general | solution.py:67
  76.2 1.9 %collective-permute-start.8 = (bf16[512,1,128]{0,2,1:T(8,128)(2,1)S(1)}, bf16[512,1,128]{0,2,1:T(8,128)(2,1)S(1)}, u32[]{:S(2)}, u32[]{:S(2)}) collective-permute-start(bf16[512,1,128]{0,2,1:T(8,128)(2,1)S(1)} %collective-permute-done.5), channel_id=1, source_target_pairs={{0,8},{8,16},{16,24},{24,32},{32,40},{40,48},{48,56},{56,64},{64,7... | collective-permute-start | bytes 393224 | tf_op jit(solution)/shard_map/ppermute | solution.py:17
  78.1 4.3 %collective-permute-done.7 = bf16[512,1,128]{2,0,1:T(8,128)(2,1)S(1)} collective-permute-done((bf16[512,1,128]{2,0,1:T(8,128)(2,1)S(1)}, bf16[512,1,128]{2,0,1:T(8,128)(2,1)S(1)}, u32[]{:S(2)}, u32[]{:S(2)}) %collective-permute-start.7) | collective-permute-done | bytes 131104 | tf_op jit(solution)/shard_map/ppermute | solution.py:17
  82.4 1.9 %collective-permute-start.10 = (bf16[512,1,128]{2,0,1:T(8,128)(2,1)S(1)}, bf16[512,1,128]{2,0,1:T(8,128)(2,1)S(1)}, u32[]{:S(2)}, u32[]{:S(2)}) collective-permute-start(bf16[512,1,128]{2,0,1:T(8,128)(2,1)S(1)} %collective-permute-done.7), channel_id=1, source_target_pairs={{0,8},{8,16},{16,24},{24,32},{32,40},{40,48},{48,56},{56,64},{64,7... | collective-permute-start | bytes 393224 | tf_op jit(solution)/shard_map/ppermute | solution.py:17
  84.3 4.7 %fusion.3 = (f32[8,512]{1,0:T(8,128)S(1)}, f32[8,512,512]{1,2,0:T(8,128)}) fusion(pred[512,512]{0,1:T(8,128)(4,1)S(1)} %get-tuple-element.145, bf16[8,512,128]{2,1,0:T(8,128)(2,1)S(1)} %maximum_bitcast_fusion, bf16[512,1,128]{2,0,1:T(8,128)(2,1)S(1)} %collective-permute-done.7), kind=kOutput, calls=%fused_computation.13 | convolution fusion | flops 543158272 | bytes 9846784 | tf_op jit(solution)/shard_map/while/body/eval_jaxpr/htd,sd->hts/dot_general | solution.py:67
  89.0 2.1 %collective-permute-start.11 = (bf16[512,1,128]{0,2,1:T(8,128)(2,1)S(1)}, bf16[512,1,128]{0,2,1:T(8,128)(2,1)S(1)}, u32[]{:S(2)}, u32[]{:S(2)}) collective-permute-start(bf16[512,1,128]{0,2,1:T(8,128)(2,1)S(1)} %collective-permute-done.8), channel_id=1, source_target_pairs={{0,8},{8,16},{16,24},{24,32},{32,40},{40,48},{48,56},{56,64},{64,7... | collective-permute-start | bytes 393224 | tf_op jit(solution)/shard_map/ppermute | solution.py:17
  91.1 1.1 collective-permute-done.10
  92.3 4.7 %fusion.4 = (f32[8,512]{1,0:T(8,128)S(1)}, f32[8,512,512]{1,2,0:T(8,128)}) fusion(pred[512,512]{0,1:T(8,128)(4,1)S(1)} %get-tuple-element.143, bf16[8,512,128]{2,1,0:T(8,128)(2,1)S(1)} %maximum_bitcast_fusion, bf16[512,1,128]{2,0,1:T(8,128)(2,1)S(1)} %collective-permute-done.10), kind=kOutput, calls=%fused_computation.14 | convolution fusion | flops 543158272 | bytes 9846784 | tf_op jit(solution)/shard_map/while/body/eval_jaxpr/htd,sd->hts/dot_general | solution.py:67
  97.0 1.7 %fusion.5 = f32[8,512]{1,0:T(8,128)S(1)} fusion(f32[8,512,512]{1,2,0:T(8,128)S(1)} %get-tuple-element.169, f32[8,512]{1,0:T(8,128)S(1)} %get-tuple-element.130, pred[512,512]{0,1:T(8,128)(4,1)S(1)} %get-tuple-element.142), kind=kLoop, calls=%fused_computation.15 | loop fusion | flops 8384512 | bytes 8683520 | tf_op jit(solution)/shard_map/while/body/eval_jaxpr/reduce_sum | solution.py:74
  98.8 3.5 %fusion.23 = f32[8,512,128]{1,2,0:T(8,128)} fusion(f32[8,512,512]{1,2,0:T(8,128)S(1)} %get-tuple-element.169, f32[8,512]{1,0:T(8,128)S(1)} %get-tuple-element.130, pred[512,512]{0,1:T(8,128)(4,1)S(1)} %get-tuple-element.142, bf16[512,128]{1,0:T(8,128)(2,1)S(1)} %copy-done), kind=kOutput, calls=%fused_computation.29 | convolution fusion | flops 545259520 | bytes 10895360 | tf_op jit(solution)/shard_map/while/body/eval_jaxpr/hts,sd->htd/dot_general | solution.py:76
  102.3 1.7 %fusion.7 = f32[8,512]{1,0:T(8,128)S(1)} fusion(f32[8,512,512]{1,2,0:T(8,128)S(1)} %get-tuple-element.167, f32[8,512]{1,0:T(8,128)S(1)} %get-tuple-element.122, pred[512,512]{0,1:T(8,128)(4,1)S(1)} %get-tuple-element.144), kind=kLoop, calls=%fused_computation.17 | loop fusion | flops 8384512 | bytes 8683520 | tf_op jit(solution)/shard_map/while/body/eval_jaxpr/reduce_sum | solution.py:74
  104.0 1.7 %fusion.9 = f32[8,512]{1,0:T(8,128)S(1)} fusion(f32[8,512,512]{1,2,0:T(8,128)S(1)} %get-tuple-element.165, f32[8,512]{1,0:T(8,128)S(1)} %get-tuple-element.121, pred[512,512]{0,1:T(8,128)(4,1)S(1)} %get-tuple-element.146), kind=kLoop, calls=%fused_computation.19 | loop fusion | flops 8384512 | bytes 8683520 | tf_op jit(solution)/shard_map/while/body/eval_jaxpr/reduce_sum | solution.py:74
  105.8 5.3 %fusion.11 = f32[8,512]{1,0:T(8,128)S(1)} fusion(f32[8,512,512]{1,2,0:T(8,128)} %get-tuple-element.152, f32[8,512]{1,0:T(8,128)S(1)} %get-tuple-element.120, pred[512,512]{0,1:T(8,128)(4,1)S(1)} %get-tuple-element.145), kind=kLoop, calls=%fused_computation.21 | loop fusion | flops 8384512 | bytes 8683520 | tf_op jit(solution)/shard_map/while/body/eval_jaxpr/reduce_sum | solution.py:74
  111.1 2.0 %fusion.13 = f32[8,512]{1,0:T(8,128)S(1)} fusion(f32[8,512,512]{1,2,0:T(8,128)S(1)} %bitcast.75, f32[8,512]{1,0:T(8,128)S(1)} %get-tuple-element.108, pred[512,512]{0,1:T(8,128)(4,1)S(1)} %get-tuple-element.143), kind=kLoop, calls=%fused_computation.23 | loop fusion | flops 8384512 | bytes 8683520 | tf_op jit(solution)/shard_map/while/body/eval_jaxpr/reduce_sum | solution.py:74
  113.0 4.9 %fusion.21 = f32[8,512,128]{1,2,0:T(8,128)} fusion(f32[8,512,512]{1,2,0:T(8,128)S(1)} %get-tuple-element.167, f32[8,512]{1,0:T(8,128)S(1)} %get-tuple-element.122, pred[512,512]{0,1:T(8,128)(4,1)S(1)} %get-tuple-element.144, bf16[512,1,128]{0,2,1:T(8,128)(2,1)} %collective-permute-done.2), kind=kOutput, calls=%fused_computation.28 | convolution fusion | flops 545259520 | bytes 10895360 | tf_op jit(solution)/shard_map/while/body/eval_jaxpr/hts,sd->htd/dot_general | solution.py:76
  118.0 2.4 %fusion.19 = f32[8,512,128]{1,2,0:T(8,128)S(1)} fusion(f32[8,512,512]{1,2,0:T(8,128)S(1)} %get-tuple-element.165, f32[8,512]{1,0:T(8,128)S(1)} %get-tuple-element.121, pred[512,512]{0,1:T(8,128)(4,1)S(1)} %get-tuple-element.146, bf16[512,1,128]{0,2,1:T(8,128)(2,1)S(1)} %collective-permute-done.5), kind=kOutput, calls=%fused_computation.27 | convolution fusion | flops 545259520 | bytes 10895360 | tf_op jit(solution)/shard_map/while/body/eval_jaxpr/hts,sd->htd/dot_general | solution.py:76
  120.4 2.4 %fusion.17 = f32[8,512,128]{1,2,0:T(8,128)S(1)} fusion(f32[8,512,512]{1,2,0:T(8,128)S(1)} %bitcast.77, f32[8,512]{1,0:T(8,128)S(1)} %get-tuple-element.120, pred[512,512]{0,1:T(8,128)(4,1)S(1)} %get-tuple-element.145, bf16[512,1,128]{0,2,1:T(8,128)(2,1)S(1)} %collective-permute-done.8), kind=kOutput, calls=%fused_computation.26 | convolution fusion | flops 545259520 | bytes 10895360 | tf_op jit(solution)/shard_map/while/body/eval_jaxpr/hts,sd->htd/dot_general | solution.py:76
  122.9 3.0 %divide_convert_fusion = bf16[8,512,128]{1,2,0:T(8,128)(2,1)S(1)} fusion(f32[8,512,128]{1,2,0:T(8,128)S(1)} %fusion.17, f32[8,512,128]{1,2,0:T(8,128)S(1)} %fusion.19, f32[8,512,128]{1,2,0:T(8,128)S(1)} %copy-done.1, f32[8,512,128]{1,2,0:T(8,128)S(1)} %copy-done.2, f32[8,512]{1,0:T(8,128)S(1)} %get-tuple-element.103, f32[8,512]{1,0:T(8,128)S(1)} %get-tuple-element.107, ...), kind=kOutput, calls=%fused_computation.43 | convolution fusion | flops 551026688 | bytes 18333696 | tf_op jit(solution)/shard_map/while/body/eval_jaxpr/hts,sd->htd/dot_general | solution.py:76
  125.9 1.3 %copy.23 = bf16[512,1024]{1,0:T(8,128)(2,1)} copy(bf16[512,1024]{0,1:T(8,128)(2,1)S(1)} %bitcast.81) | data formatting | bytes 2097152 | tf_op jit(solution)/shard_map/convert_element_type | solution.py:92
  (34 shorter events, 0.5 us)
Async XLA Ops:
  14.5 17.8 %collective-permute-start = (bf16[512]{0:T(512)(128)(2,1)S(1)}, bf16[512]{0:T(512)(128)(2,1)}, u32[]{:S(2)}, u32[]{:S(2)}) collective-permute-start(bf16[512]{0:T(512)(128)(2,1)S(1)} %convert_element_type.73), channel_id=1, source_target_pairs={{0,8},{8,16},{16,24},{24,32},{32,40},{40,48},{48,56},{56,64},{64,7... | collective-permute-start | bytes 3080 | tf_op jit(solution)/shard_map/ppermute | solution.py:17
  19.4 43.2 %collective-permute-start.1 = (bf16[512,1,128]{2,0,1:T(8,128)(2,1)}, bf16[512,1,128]{2,0,1:T(8,128)(2,1)S(1)}, u32[]{:S(2)}, u32[]{:S(2)}) collective-permute-start(bf16[512,1,128]{2,0,1:T(8,128)(2,1)} %pad_maximum_fusion), channel_id=1, source_target_pairs={{0,8},{8,16},{16,24},{24,32},{32,40},{40,48},{48,56},{56,64},{64,7... | collective-permute-start | bytes 393224 | tf_op jit(solution)/shard_map/ppermute | solution.py:17
  25.0 41.1 %collective-permute-start.2 = (bf16[512,1,128]{0,2,1:T(8,128)(2,1)}, bf16[512,1,128]{0,2,1:T(8,128)(2,1)}, u32[]{:S(2)}, u32[]{:S(2)}) collective-permute-start(bf16[512,1,128]{0,2,1:T(8,128)(2,1)} %bitcast.14), channel_id=1, source_target_pairs={{0,8},{8,16},{16,24},{24,32},{32,40},{40,48},{48,56},{56,64},{64,7... | collective-permute-start | bytes 393224 | tf_op jit(solution)/shard_map/ppermute | solution.py:17
  32.4 8.7 %collective-permute-start.3 = (bf16[512]{0:T(512)(128)(2,1)}, bf16[512]{0:T(512)(128)(2,1)S(1)}, u32[]{:S(2)}, u32[]{:S(2)}) collective-permute-start(bf16[512]{0:T(512)(128)(2,1)} %collective-permute-done), channel_id=1, source_target_pairs={{0,8},{8,16},{16,24},{24,32},{32,40},{40,48},{48,56},{56,64},{64,7... | collective-permute-start | bytes 3080 | tf_op jit(solution)/shard_map/ppermute | solution.py:17
  41.1 8.5 %collective-permute-start.6 = (bf16[512]{0:T(512)(128)(2,1)S(1)}, bf16[512]{0:T(512)(128)(2,1)S(1)}, u32[]{:S(2)}, u32[]{:S(2)}) collective-permute-start(bf16[512]{0:T(512)(128)(2,1)S(1)} %collective-permute-done.3), channel_id=1, source_target_pairs={{0,8},{8,16},{16,24},{24,32},{32,40},{40,48},{48,56},{56,64},{64,7... | collective-permute-start | bytes 3080 | tf_op jit(solution)/shard_map/ppermute | solution.py:17
  49.6 8.5 %collective-permute-start.9 = (bf16[512]{0:T(512)(128)(2,1)S(1)}, bf16[512]{0:T(512)(128)(2,1)S(1)}, u32[]{:S(2)}, u32[]{:S(2)}) collective-permute-start(bf16[512]{0:T(512)(128)(2,1)S(1)} %collective-permute-done.6), channel_id=1, source_target_pairs={{0,8},{8,16},{16,24},{24,32},{32,40},{40,48},{48,56},{56,64},{64,7... | collective-permute-start | bytes 3080 | tf_op jit(solution)/shard_map/ppermute | solution.py:17
  62.6 9.9 %collective-permute-start.4 = (bf16[512,1,128]{2,0,1:T(8,128)(2,1)S(1)}, bf16[512,1,128]{2,0,1:T(8,128)(2,1)S(1)}, u32[]{:S(2)}, u32[]{:S(2)}) collective-permute-start(bf16[512,1,128]{2,0,1:T(8,128)(2,1)S(1)} %collective-permute-done.1), channel_id=1, source_target_pairs={{0,8},{8,16},{16,24},{24,32},{32,40},{40,48},{48,56},{56,64},{64,7... | collective-permute-start | bytes 393224 | tf_op jit(solution)/shard_map/ppermute | solution.py:17
  66.1 10.1 %collective-permute-start.5 = (bf16[512,1,128]{0,2,1:T(8,128)(2,1)}, bf16[512,1,128]{0,2,1:T(8,128)(2,1)S(1)}, u32[]{:S(2)}, u32[]{:S(2)}) collective-permute-start(bf16[512,1,128]{0,2,1:T(8,128)(2,1)} %collective-permute-done.2), channel_id=1, source_target_pairs={{0,8},{8,16},{16,24},{24,32},{32,40},{40,48},{48,56},{56,64},{64,7... | collective-permute-start | bytes 393224 | tf_op jit(solution)/shard_map/ppermute | solution.py:17
  72.5 9.9 %collective-permute-start.7 = (bf16[512,1,128]{2,0,1:T(8,128)(2,1)S(1)}, bf16[512,1,128]{2,0,1:T(8,128)(2,1)S(1)}, u32[]{:S(2)}, u32[]{:S(2)}) collective-permute-start(bf16[512,1,128]{2,0,1:T(8,128)(2,1)S(1)} %collective-permute-done.4), channel_id=1, source_target_pairs={{0,8},{8,16},{16,24},{24,32},{32,40},{40,48},{48,56},{56,64},{64,7... | collective-permute-start | bytes 393224 | tf_op jit(solution)/shard_map/ppermute | solution.py:17
  76.2 12.8 %collective-permute-start.8 = (bf16[512,1,128]{0,2,1:T(8,128)(2,1)S(1)}, bf16[512,1,128]{0,2,1:T(8,128)(2,1)S(1)}, u32[]{:S(2)}, u32[]{:S(2)}) collective-permute-start(bf16[512,1,128]{0,2,1:T(8,128)(2,1)S(1)} %collective-permute-done.5), channel_id=1, source_target_pairs={{0,8},{8,16},{16,24},{24,32},{32,40},{40,48},{48,56},{56,64},{64,7... | collective-permute-start | bytes 393224 | tf_op jit(solution)/shard_map/ppermute | solution.py:17
  82.4 9.9 %collective-permute-start.10 = (bf16[512,1,128]{2,0,1:T(8,128)(2,1)S(1)}, bf16[512,1,128]{2,0,1:T(8,128)(2,1)S(1)}, u32[]{:S(2)}, u32[]{:S(2)}) collective-permute-start(bf16[512,1,128]{2,0,1:T(8,128)(2,1)S(1)} %collective-permute-done.7), channel_id=1, source_target_pairs={{0,8},{8,16},{16,24},{24,32},{32,40},{40,48},{48,56},{56,64},{64,7... | collective-permute-start | bytes 393224 | tf_op jit(solution)/shard_map/ppermute | solution.py:17
  89.0 33.9 %collective-permute-start.11 = (bf16[512,1,128]{0,2,1:T(8,128)(2,1)S(1)}, bf16[512,1,128]{0,2,1:T(8,128)(2,1)S(1)}, u32[]{:S(2)}, u32[]{:S(2)}) collective-permute-start(bf16[512,1,128]{0,2,1:T(8,128)(2,1)S(1)} %collective-permute-done.8), channel_id=1, source_target_pairs={{0,8},{8,16},{16,24},{24,32},{32,40},{40,48},{48,56},{56,64},{64,7... | collective-permute-start | bytes 393224 | tf_op jit(solution)/shard_map/ppermute | solution.py:17
  92.3 6.5 %copy-start = (bf16[512,128]{1,0:T(8,128)(2,1)S(1)}, bf16[512,128]{1,0:T(8,128)(2,1)}, u32[]{:S(2)}) copy-start(bf16[512,128]{1,0:T(8,128)(2,1)} %param.6) | copy-start | bytes 393220
  104.0 7.0 %slice-start = ((s8[8388608]{0:T(1024)(128)(4,1)}), s8[4194304]{0:T(1024)(128)(4,1)S(1)}, s32[]{:S(2)}) async-start(s8[8388608]{0:T(1024)(128)(4,1)} %bitcast.74), calls=%async_computation | async-start | bytes 8388608
  105.8 5.3 %slice-start.1 = ((s8[8388608]{0:T(1024)(128)(4,1)}), s8[4194304]{0:T(1024)(128)(4,1)S(1)}, s32[]{:S(2)}) async-start(s8[8388608]{0:T(1024)(128)(4,1)} %bitcast.74), calls=%async_computation.1 | async-start | bytes 8388608
  113.0 7.3 %slice-start.2 = ((s8[8388608]{0:T(1024)(128)(4,1)}), s8[4194304]{0:T(1024)(128)(4,1)S(1)}, s32[]{:S(2)}) async-start(s8[8388608]{0:T(1024)(128)(4,1)} %bitcast.76), calls=%async_computation.2 | async-start | bytes 8388608
  118.0 2.4 %slice-start.3 = ((s8[8388608]{0:T(1024)(128)(4,1)}), s8[4194304]{0:T(1024)(128)(4,1)S(1)}, s32[]{:S(2)}) async-start(s8[8388608]{0:T(1024)(128)(4,1)} %bitcast.76), calls=%async_computation.3 | async-start | bytes 8388608
  120.4 2.5 %copy-start.1 = (f32[8,512,128]{1,2,0:T(8,128)S(1)}, f32[8,512,128]{1,2,0:T(8,128)}, u32[]{:S(2)}) copy-start(f32[8,512,128]{1,2,0:T(8,128)} %fusion.21) | copy-start | bytes 6291460
  120.4 2.5 %copy-start.2 = (f32[8,512,128]{1,2,0:T(8,128)S(1)}, f32[8,512,128]{1,2,0:T(8,128)}, u32[]{:S(2)}) copy-start(f32[8,512,128]{1,2,0:T(8,128)} %fusion.23) | copy-start | bytes 6291460
where the time goes:
time: 128 us; the launch traced here: 127 us
  matrix products  30.4 us (24%)
  waiting for transfers between devices  28 us (22%)
  starting transfers between devices  27.1 us (21%)
  other arithmetic  21.2 us (17%)
  blocking collectives  11.7 us (9%)
  local copies, waits for them, and re-layouts  7.67 us (6%)
    ppermute x12, waiting for transfers between devices, shifted(): lax.ppermute(value, axis, [(source, source + steps) for source in range(l...  28 us
    ppermute x12, starting transfers between devices, shifted(): lax.ppermute(value, axis, [(source, source + steps) for source in range(l...  27.1 us
    dot_general x5, matrix products, one_head(): jnp.einsum('hts,sd->htd', rounded, vgroup, preferred_element_type=jnp.flo...  16.2 us
    dot_general x5, matrix products, one_head(): jnp.einsum('htd,sd->hts', qgroup, kgroup, preferred_element_type=jnp.floa...  14.2 us
    reduce_sum x5, other arithmetic, one_head(): total = total * factor + jnp.sum(weights, axis=-1)  12.5 us
    unnamed x1, blocking collectives  11.7 us
    unnamed x21, local copies, waits for them, and re-layouts  6.26 us
    and x1, other arithmetic, absorb(): visible & (token_positions[:, None] - key_pos[None, :] < window)  2.9 us
  transfers between devices with their start and end apart: 12, of which 7 were waited for; matrix products, arithmetic and copies ran while one was open for 41% of the time, Pallas kernels for 0%

commit v1 on v0

v1 whole, which is shorter than its diff:
```python
import functools

import jax
import jax.numpy as jnp
import numpy as np
from jax import lax
from jax.experimental import pallas as pl
from jax.experimental.pallas import tpu as pltpu
from jax.sharding import PartitionSpec as P

HEAD = 128
GROUP = 8
TOK = 512
N_CTX = 32
THETA = 1000000.0
NEG = -1e30
SCALE = float(np.log2(np.e) / np.sqrt(HEAD))
TQ = 128


def rotary_table():
    half = HEAD // 2
    inv = np.float32(THETA) ** (-(np.float32(2.0) * np.arange(half, dtype=np.float32)) / np.float32(HEAD))
    angle = np.arange(N_CTX * TOK, dtype=np.float32)[:, None] * inv.astype(np.float32)[None, :]
    wide = angle.astype(np.float64)
    table = np.concatenate([np.cos(wide), np.sin(wide)], axis=1).astype(np.float32)
    return table.reshape(N_CTX, TOK, HEAD)


def wide_factors(table):
    turned = pltpu.roll(table, HEAD // 2, 1)
    low = lax.broadcasted_iota(jnp.int32, table.shape, 1) < HEAD // 2
    return jnp.where(low, table, turned), jnp.where(low, -turned, table)


def rotate(x, cosine, sine):
    x = x.astype(jnp.float32)
    return (x * cosine + pltpu.roll(x, HEAD // 2, 1) * sine).astype(jnp.bfloat16)


def pack_kernel(ctx_ref, table_ref, k_ref, v_ref, out_ref):
    cosine, sine = wide_factors(table_ref[0])
    out_ref[:, :HEAD] = rotate(k_ref[...], cosine, sine)
    out_ref[:, HEAD:] = v_ref[...]


def twice(x):
    return jnp.concatenate([x, x], axis=1)


def prepare_block(kv_ref, kt, va, slot):
    kt[slot] = kv_ref[:, :HEAD].T
    va[slot, :, :HEAD] = kv_ref[:, HEAD:]
    va[slot, :, HEAD:] = jnp.ones((TOK, HEAD), jnp.bfloat16)


def far_tile(row, q, kt, va, slot, start, count, base, m_ref, acc_ref):
    rows = pl.ds(row, TQ)
    kpos = base + lax.broadcasted_iota(jnp.int32, (1, TOK), 1)
    key_bias = jnp.where(kpos >= start, 0.0, NEG)
    live = row + lax.broadcasted_iota(jnp.int32, (TQ, HEAD), 0) < count
    for h in range(GROUP):
        s = jnp.dot(q[h, rows, :], kt[slot], preferred_element_type=jnp.float32)
        s = s * SCALE + key_bias
        old = m_ref[h, rows, :]
        top = jnp.where(live, jnp.max(s, axis=1, keepdims=True), NEG)
        new = jnp.maximum(old, top)
        shift = jnp.where(live, new, -NEG)
        p = jnp.exp2(s - jnp.concatenate([shift] * (TOK // HEAD), axis=1))
        factor = jnp.exp2(old - new)
        m_ref[h, rows, :] = new
        update = jnp.dot(p.astype(jnp.bfloat16), va[slot], preferred_element_type=jnp.float32)
        acc_ref[h, rows, :] = acc_ref[h, rows, :] * twice(factor) + update


def far_blocks(bases, ctx_base, q, kt, va, start, count, m_ref, acc_ref):
    for slot, base in enumerate(bases):

        @pl.when((base < ctx_base) & (base + TOK > start))
        def _():
            def body(i, carry):
                far_tile(pl.multiple_of(i * TQ, TQ), q, kt, va, slot, start, count, base, m_ref, acc_ref)
                return carry

            lax.fori_loop(0, (count + TQ - 1) // TQ, body, 0)


def rotate_queries(q_ref, table_ref, q):
    cosine, sine = wide_factors(table_ref[0])
    for h in range(GROUP):
        q[h] = rotate(q_ref[:, h * HEAD : (h + 1) * HEAD], cosine, sine)


def document(ids, ids1, ids2, ctx):
    own = jnp.sum(ids[:8], axis=0, keepdims=True)
    first = own[:, :1]

    def matches(block):
        return jnp.sum(jnp.where(jnp.sum(block, axis=0, keepdims=True) == first, 1, 0))

    before = matches(ids[8:]) * lax.rem(ctx, 2)
    for other in (ids1, ids2):
        before = before + matches(other[:8]) + matches(other[8:])
    return own, ctx * TOK - before, matches(ids[:8])


def first_kernel(
    ctx_ref, table_ref, q_ref, own_ref, sib_ref, r1_ref, r1s_ref, ids_ref, ids1_ref, ids2_ref,
    m_out, acc_out, q, kt, va, bias,
):
    ctx = ctx_ref[0]
    other = ctx + 1 - 2 * lax.rem(ctx, 2)
    rotate_queries(q_ref, table_ref, q)
    own, start, count = document(ids_ref[...], ids1_ref[...], ids2_ref[...], ctx)
    for slot, ref in enumerate((own_ref, sib_ref, r1_ref, r1s_ref)):
        prepare_block(ref, kt, va, slot)
    column = jnp.broadcast_to(own, (HEAD, TOK)).T
    for t in range(TOK // TQ):
        rows = slice(t * TQ, (t + 1) * TQ)
        width = (t + 1) * TQ
        key = lax.broadcasted_iota(jnp.int32, (TQ, width), 1)
        query = t * TQ + lax.broadcasted_iota(jnp.int32, (TQ, width), 0)
        same = jnp.concatenate([column[rows]] * (width // HEAD), axis=1) == own[:, :width]
        bias[:, :width] = jnp.where(same & (key <= query), 0.0, NEG)
        for h in range(GROUP):
            s = jnp.dot(q[h, rows, :], kt[0, :, :width], preferred_element_type=jnp.float32)
            s = s * SCALE + bias[:, :width]
            top = jnp.broadcast_to(jnp.max(s, axis=1, keepdims=True), (TQ, HEAD))
            p = jnp.exp2(s - jnp.concatenate([top] * (width // HEAD), axis=1))
            m_out[h, rows, :] = top
            acc_out[h, rows, :] = jnp.dot(
                p.astype(jnp.bfloat16), va[0, :width, :], preferred_element_type=jnp.float32
            )
    bases = [other * TOK, (ctx - 2) * TOK, (other - 2) * TOK]
    far_blocks(bases, ctx * TOK, q, kt.at[1:], va.at[1:], start, count, m_out, acc_out)


def last_kernel(
    ctx_ref, table_ref, q_ref, r2_ref, r2s_ref, ids_ref, ids1_ref, ids2_ref, m_in, acc_in,
    out_ref, q, kt, va,
):
    ctx = ctx_ref[0]
    other = ctx + 1 - 2 * lax.rem(ctx, 2)
    _, start, count = document(ids_ref[...], ids1_ref[...], ids2_ref[...], ctx)
    bases = [(ctx - 4) * TOK, (other - 4) * TOK]

    @pl.when(start < jnp.maximum(bases[0], bases[1]) + TOK)
    def _():
        rotate_queries(q_ref, table_ref, q)
        for slot, ref in enumerate((r2_ref, r2s_ref)):
            prepare_block(ref, kt, va, slot)
        far_blocks(bases, ctx * TOK, q, kt, va, start, count, m_in, acc_in)

    for h in range(GROUP):
        acc = acc_in[h]
        out_ref[:, h * HEAD : (h + 1) * HEAD] = (acc[:, :HEAD] / acc[:, HEAD:]).astype(jnp.bfloat16)


def whole(shape):
    return pl.BlockSpec(shape, lambda i, ctx: (0,) * len(shape))


TABLE_SPEC = pl.BlockSpec((1, TOK, HEAD), lambda i, ctx: (ctx[0], 0, 0))
KV = (TOK, 2 * HEAD)
STATE = ((GROUP, TOK, HEAD), (GROUP, TOK, 2 * HEAD))
LIMIT = 48 * 2**20


def call(kernel, name, ins, outs, dtypes, scratch, flops):
    return pl.pallas_call(
        kernel,
        grid_spec=pltpu.PrefetchScalarGridSpec(
            num_scalar_prefetch=1,
            grid=(1,),
            in_specs=[TABLE_SPEC] + [whole(s) for s in ins],
            out_specs=[whole(s) for s in outs],
            scratch_shapes=scratch,
        ),
        out_shape=[jax.ShapeDtypeStruct(s, d) for s, d in zip(outs, dtypes)],
        compiler_params=pltpu.CompilerParams(vmem_limit_bytes=LIMIT),
        cost_estimate=pl.CostEstimate(flops=flops, bytes_accessed=2**21, transcendentals=0),
        name=name,
    )


def blocks_scratch(count):
    return [
        pltpu.VMEM((GROUP, TOK, HEAD), jnp.bfloat16),
        pltpu.VMEM((count, HEAD, TOK), jnp.bfloat16),
        pltpu.VMEM((count, TOK, 2 * HEAD), jnp.bfloat16),
    ]


def shifted(value, steps):
    return lax.ppermute(value, "ctx", [(i, i + steps) for i in range(N_CTX - steps)])


def swapped(value):
    return lax.ppermute(value, "ctx", [(i, i ^ 1) for i in range(N_CTX)])


def local(q_proj, key_projection, value_projection, doc_ids):
    table = jnp.asarray(rotary_table())
    index = lax.axis_index("ctx").astype(jnp.int32)
    ctx = index.reshape(1)
    place = lax.axis_index("kvh")
    spread = jnp.where(
        jnp.arange(TOK, dtype=jnp.int32) // doc_ids.shape[0] == place, jnp.tile(doc_ids, 8) + 1, 0
    ).astype(jnp.float32)
    ids = lax.all_to_all(jnp.broadcast_to(spread, (8, TOK)), "kvh", 0, 0, tiled=True)
    (own,) = call(pack_kernel, "pack", [(TOK, HEAD)] * 2, [KV], [jnp.bfloat16], [], 10**6)(
        ctx, table, key_projection, value_projection
    )
    sib = swapped(own)
    r1 = shifted(own, 2)
    r1s = swapped(r1)
    r2 = shifted(r1, 2)
    r2s = swapped(r2)
    both = jnp.concatenate([ids, swapped(ids)], axis=0)
    ids1 = shifted(both, 2)
    ids2 = shifted(both, 4)
    m, acc = call(
        first_kernel,
        "first",
        [(TOK, GROUP * HEAD)] + [KV] * 4 + [(16, TOK)] * 3,
        list(STATE),
        [jnp.float32] * 2,
        blocks_scratch(4) + [pltpu.VMEM((TQ, TOK), jnp.float32)],
        10**10,
    )(ctx, table, q_proj, own, sib, r1, r1s, both, ids1, ids2)
    (out,) = call(
        last_kernel,
        "last",
        [(TOK, GROUP * HEAD)] + [KV] * 2 + [(16, TOK)] * 3 + list(STATE),
        [(TOK, GROUP * HEAD)],
        [jnp.bfloat16],
        blocks_scratch(2),
        4 * 10**9,
    )(ctx, table, q_proj, r2, r2s, both, ids1, ids2, m, acc)
    return out


def solution(mesh):
    in_specs = (P("ctx", "kvh"), P("ctx", "kvh"), P("ctx", "kvh"), P(("ctx", "kvh")))
    return jax.shard_map(
        local, mesh=mesh, in_specs=in_specs, out_specs=P("ctx", "kvh"), check_vma=False
    )
```

time: 128 us -> 69.7 us (0.54)
  the two profiles are of different devices: /device:TPU:16 before, /device:TPU:49 now
where the time goes in v1:
time: 69.7 us; the launch traced here: 69.4 us
  Pallas kernels  27.5 us (39%)
  starting transfers between devices  21.3 us (31%)
  blocking collectives  9.6 us (14%)
  waiting for transfers between devices  8.97 us (13%)
  local copies, waits for them, and re-layouts  1.91 us (3%)
    pallas_call x1, Pallas kernels, local(): call(first_kernel, 'first', [(TOK, GROUP * HEAD)] + [KV] * 4 + [(16, TOK)...  18.2 us
    ppermute x4, starting transfers between devices, shifted(): lax.ppermute(value, 'ctx', [(i, i + steps) for i in range(N_CTX - steps)])  16.3 us
    all_to_all x1, blocking collectives, local(): lax.all_to_all(jnp.broadcast_to(spread, (8, TOK)), 'kvh', 0, 0, tiled=True)  9.6 us
    ppermute x4, waiting for transfers between devices, shifted(): lax.ppermute(value, 'ctx', [(i, i + steps) for i in range(N_CTX - steps)])  8.13 us
    pallas_call x1, Pallas kernels, local(): call(last_kernel, 'last', [(TOK, GROUP * HEAD)] + [KV] * 2 + [(16, TOK)]...  8.1 us
    ppermute x4, starting transfers between devices, swapped(): return lax.ppermute(value, 'ctx', [(i, i ^ 1) for i in range(N_CTX)])  5.01 us
    unnamed x9, local copies, waits for them, and re-layouts  1.82 us
  transfers between devices with their start and end apart: 8, of which 3 were waited for; matrix products, arithmetic and copies ran while one was open for 0% of the time, Pallas kernels for 26%

profile of v1, /device:TPU:49, one launch (start us, length us, event | category | flops | bytes accessed | tf_op | source)
XLA Modules:
  0.0 69.4 jit_solution(10025075034142075590)
XLA Ops:
  0.0 0.0 copy-start.1
  0.0 0.9 %copy-done.1 = bf16[512,128]{1,0:T(8,128)(2,1)S(1)} copy-done((bf16[512,128]{1,0:T(8,128)(2,1)S(1)}, bf16[512,128]{1,0:T(8,128)(2,1)}, u32[]{:S(2)}) %copy-start.1) | copy-done | bytes 131096
  0.9 0.0 copy-start.2
  0.9 0.9 %copy-done.2 = bf16[512,128]{1,0:T(8,128)(2,1)S(1)} copy-done((bf16[512,128]{1,0:T(8,128)(2,1)S(1)}, bf16[512,128]{1,0:T(8,128)(2,1)}, u32[]{:S(2)}) %copy-start.2) | copy-done | bytes 131096
  1.8 0.0 copy-start.3
  1.8 0.0 copy-start
  1.8 1.2 %pack.1.own_ref = bf16[512,256]{1,0:T(8,128)(2,1)S(1)} custom-call(s32[1]{0:T(128)} %bitcast.ctx_ref, f32[32,512,128]{2,1,0:T(8,128)} %constant.31.clone.table_ref, bf16[512,128]{1,0:T(8,128)(2,1)S(1)} %copy-done.1, bf16[512,128]{1,0:T(8,128)(2,1)S(1)} %copy-done.2), custom_call_target="tpu_custom_call" | custom-call | flops 1000000 | bytes 2097152 | tf_op jit(solution)/shard_map/pack/pallas_call | solution.py:211
  3.1 3.5 %collective-permute-start = (bf16[512,256]{1,0:T(8,128)(2,1)S(1)}, bf16[512,256]{1,0:T(8,128)(2,1)S(1)}, u32[]{:S(2)}, u32[]{:S(2)}) collective-permute-start(bf16[512,256]{1,0:T(8,128)(2,1)S(1)} %pack.1.own_ref), channel_id=1, source_target_pairs={{0,16},{8,24},{16,32},{24,40},{32,48},{40,56},{48,64},{56,72},{64,... | collective-permute-start | bytes 786440 | tf_op jit(solution)/shard_map/ppermute | solution.py:195
  6.6 1.0 %collective-permute-start.6 = (bf16[512,256]{1,0:T(8,128)(2,1)S(1)}, bf16[512,256]{1,0:T(8,128)(2,1)S(1)}, u32[]{:S(2)}, u32[]{:S(2)}) collective-permute-start(bf16[512,256]{1,0:T(8,128)(2,1)S(1)} %pack.1.own_ref), channel_id=1, source_target_pairs={{0,8},{8,0},{16,24},{24,16},{32,40},{40,32},{48,56},{56,48},{64,72... | collective-permute-start | bytes 786440 | tf_op jit(solution)/shard_map/ppermute | solution.py:199
  7.7 0.0 copy-done.3
  7.7 0.1 add.10
  7.7 4.4 %collective-permute-done.r1_ref = bf16[512,256]{1,0:T(8,128)(2,1)S(1)} collective-permute-done((bf16[512,256]{1,0:T(8,128)(2,1)S(1)}, bf16[512,256]{1,0:T(8,128)(2,1)S(1)}, u32[]{:S(2)}, u32[]{:S(2)}) %collective-permute-start) | collective-permute-done | bytes 262176 | tf_op jit(solution)/shard_map/ppermute | solution.py:195
  12.1 1.5 %collective-permute-start.7 = (bf16[512,256]{1,0:T(8,128)(2,1)S(1)}, bf16[512,256]{1,0:T(8,128)(2,1)S(1)}, u32[]{:S(2)}, u32[]{:S(2)}) collective-permute-start(bf16[512,256]{1,0:T(8,128)(2,1)S(1)} %collective-permute-done.r1_ref), channel_id=1, source_target_pairs={{0,8},{8,0},{16,24},{24,16},{32,40},{40,32},{48,56},{56,48},{64,72... | collective-permute-start | bytes 786440 | tf_op jit(solution)/shard_map/ppermute | solution.py:199
  13.7 3.5 %collective-permute-start.1 = (bf16[512,256]{1,0:T(8,128)(2,1)S(1)}, bf16[512,256]{1,0:T(8,128)(2,1)S(1)}, u32[]{:S(2)}, u32[]{:S(2)}) collective-permute-start(bf16[512,256]{1,0:T(8,128)(2,1)S(1)} %collective-permute-done.r1_ref), channel_id=1, source_target_pairs={{0,16},{8,24},{16,32},{24,40},{32,48},{40,56},{48,64},{56,72},{64,... | collective-permute-start | bytes 786440 | tf_op jit(solution)/shard_map/ppermute | solution.py:195
  17.3 9.6 %all_to_all.9 = f32[8,1,512]{2,1,0:T(1,128)S(1)} all-to-all(f32[8,1,512]{2,1,0:T(1,128)S(1)} %broadcast_in_dim.5), channel_id=1, replica_groups=mesh['ctx'=32,'kvh'=8] {'kvh'}, dimensions={0} | all-to-all | bytes 32768 | tf_op jit(solution)/shard_map/all_to_all | solution.py:210
  26.9 1.7 %collective-permute-start.3 = (f32[8,512]{1,0:T(8,128)S(1)}, f32[8,512]{1,0:T(8,128)S(1)}, u32[]{:S(2)}, u32[]{:S(2)}) collective-permute-start(f32[8,512]{1,0:T(8,128)S(1)} %bitcast.4), channel_id=1, source_target_pairs={{0,8},{8,0},{16,24},{24,16},{32,40},{40,32},{48,56},{56,48},{64,72... | collective-permute-start | bytes 49160 | tf_op jit(solution)/shard_map/ppermute | solution.py:199
  28.6 0.8 %collective-permute-done.3 = f32[8,512]{1,0:T(8,128)S(1)} collective-permute-done((f32[8,512]{1,0:T(8,128)S(1)}, f32[8,512]{1,0:T(8,128)S(1)}, u32[]{:S(2)}, u32[]{:S(2)}) %collective-permute-start.3) | collective-permute-done | bytes 16416 | tf_op jit(solution)/shard_map/ppermute | solution.py:199
  29.4 4.2 %collective-permute-start.4 = (f32[16,512]{1,0:T(8,128)S(1)}, f32[16,512]{1,0:T(8,128)S(1)}, u32[]{:S(2)}, u32[]{:S(2)}) collective-permute-start(f32[16,512]{1,0:T(8,128)S(1)} %pad_maximum_fusion.ids_ref), channel_id=1, source_target_pairs={{0,16},{8,24},{16,32},{24,40},{32,48},{40,56},{48,64},{56,72},{64,... | collective-permute-start | bytes 98312 | tf_op jit(solution)/shard_map/ppermute | solution.py:195
  33.6 5.0 %collective-permute-start.5 = (f32[16,512]{1,0:T(8,128)S(1)}, f32[16,512]{1,0:T(8,128)S(1)}, u32[]{:S(2)}, u32[]{:S(2)}) collective-permute-start(f32[16,512]{1,0:T(8,128)S(1)} %pad_maximum_fusion.ids_ref), channel_id=1, source_target_pairs={{0,32},{8,40},{16,48},{24,56},{32,64},{40,72},{48,80},{56,88},{64,... | collective-permute-start | bytes 98312 | tf_op jit(solution)/shard_map/ppermute | solution.py:195
  38.7 0.0 collective-permute-done.1.r2_ref
  38.7 0.7 %collective-permute-start.2 = (bf16[512,256]{1,0:T(8,128)(2,1)S(1)}, bf16[512,256]{1,0:T(8,128)(2,1)S(1)}, u32[]{:S(2)}, u32[]{:S(2)}) collective-permute-start(bf16[512,256]{1,0:T(8,128)(2,1)S(1)} %collective-permute-done.1.r2_ref), channel_id=1, source_target_pairs={{0,8},{8,0},{16,24},{24,16},{32,40},{40,32},{48,56},{56,48},{64,72... | collective-permute-start | bytes 786440 | tf_op jit(solution)/shard_map/ppermute | solution.py:199
  39.4 0.0 collective-permute-done.4.ids1_ref
  39.4 3.7 %collective-permute-done.5.ids2_ref = f32[16,512]{1,0:T(8,128)S(1)} collective-permute-done((f32[16,512]{1,0:T(8,128)S(1)}, f32[16,512]{1,0:T(8,128)S(1)}, u32[]{:S(2)}, u32[]{:S(2)}) %collective-permute-start.5) | collective-permute-done | bytes 32800 | tf_op jit(solution)/shard_map/ppermute | solution.py:195
  43.1 0.0 collective-permute-done.6.sib_ref
  43.1 0.0 collective-permute-done.7.r1s_ref
  43.1 0.0 copy-done
  43.1 18.2 %first.1 = (f32[8,512,128]{2,1,0:T(8,128)S(1)}, f32[8,512,256]{2,1,0:T(8,128)}) custom-call(s32[1]{0:T(128)} %bitcast.ctx_ref, f32[32,512,128]{2,1,0:T(8,128)} %constant.31.clone.table_ref, bf16[512,1024]{1,0:T(8,128)(2,1)S(1)} %copy-done, bf16[512,256]{1,0:T(8,128)(2,1)S(1)} %pack.1.own_ref, bf16[512,256]{1,0:T(8,128)(2,1)S(1)} %collective-permute-done.6.sib_ref, ...), custom_call_target="tpu_custom_call" | custom-call | flops 10000000000 | bytes 2097152 | tf_op jit(solution)/shard_map/first/pallas_call | solution.py:222
  61.3 0.0 collective-permute-done.2.r2s_ref
  61.3 8.1 %last.1 = bf16[512,1024]{1,0:T(8,128)(2,1)} custom-call(s32[1]{0:T(128)} %bitcast.ctx_ref, f32[32,512,128]{2,1,0:T(8,128)} %constant.31.clone.table_ref, bf16[512,1024]{1,0:T(8,128)(2,1)S(1)} %copy-done, bf16[512,256]{1,0:T(8,128)(2,1)S(1)} %collective-permute-done.1.r2_ref, bf16[512,256]{1,0:T(8,128)(2,1)S(1)} %collective-permute-done.2.r2s_ref, ...), custom_call_target="tpu_custom_call" | custom-call | flops 4000000000 | bytes 2097152 | tf_op jit(solution)/shard_map/last/pallas_call | solution.py:231
  (6 shorter events, 0.0 us)
Async XLA Ops:
  0.0 0.9 %copy-start.1 = (bf16[512,128]{1,0:T(8,128)(2,1)S(1)}, bf16[512,128]{1,0:T(8,128)(2,1)}, u32[]{:S(2)}) copy-start(bf16[512,128]{1,0:T(8,128)(2,1)} %k_ref.1) | copy-start | bytes 393220
  0.9 0.9 %copy-start.2 = (bf16[512,128]{1,0:T(8,128)(2,1)S(1)}, bf16[512,128]{1,0:T(8,128)(2,1)}, u32[]{:S(2)}) copy-start(bf16[512,128]{1,0:T(8,128)(2,1)} %v_ref.1) | copy-start | bytes 393220
  1.8 5.8 %copy-start.3 = (s32[64]{0:T(128)S(1)}, s32[64]{0:T(128)}, u32[]{:S(2)}) copy-start(s32[64]{0:T(128)} %param.8) | copy-start | bytes 772
  1.8 41.3 %copy-start = (bf16[512,1024]{1,0:T(8,128)(2,1)S(1)}, bf16[512,1024]{1,0:T(8,128)(2,1)}, u32[]{:S(2)}) copy-start(bf16[512,1024]{1,0:T(8,128)(2,1)} %q_ref.3) | copy-start | bytes 3145732
  3.1 9.1 %collective-permute-start = (bf16[512,256]{1,0:T(8,128)(2,1)S(1)}, bf16[512,256]{1,0:T(8,128)(2,1)S(1)}, u32[]{:S(2)}, u32[]{:S(2)}) collective-permute-start(bf16[512,256]{1,0:T(8,128)(2,1)S(1)} %pack.1.own_ref), channel_id=1, source_target_pairs={{0,16},{8,24},{16,32},{24,40},{32,48},{40,56},{48,64},{56,72},{64,... | collective-permute-start | bytes 786440 | tf_op jit(solution)/shard_map/ppermute | solution.py:195
  6.6 36.5 %collective-permute-start.6 = (bf16[512,256]{1,0:T(8,128)(2,1)S(1)}, bf16[512,256]{1,0:T(8,128)(2,1)S(1)}, u32[]{:S(2)}, u32[]{:S(2)}) collective-permute-start(bf16[512,256]{1,0:T(8,128)(2,1)S(1)} %pack.1.own_ref), channel_id=1, source_target_pairs={{0,8},{8,0},{16,24},{24,16},{32,40},{40,32},{48,56},{56,48},{64,72... | collective-permute-start | bytes 786440 | tf_op jit(solution)/shard_map/ppermute | solution.py:199
  12.1 31.0 %collective-permute-start.7 = (bf16[512,256]{1,0:T(8,128)(2,1)S(1)}, bf16[512,256]{1,0:T(8,128)(2,1)S(1)}, u32[]{:S(2)}, u32[]{:S(2)}) collective-permute-start(bf16[512,256]{1,0:T(8,128)(2,1)S(1)} %collective-permute-done.r1_ref), channel_id=1, source_target_pairs={{0,8},{8,0},{16,24},{24,16},{32,40},{40,32},{48,56},{56,48},{64,72... | collective-permute-start | bytes 786440 | tf_op jit(solution)/shard_map/ppermute | solution.py:199
  13.7 25.0 %collective-permute-start.1 = (bf16[512,256]{1,0:T(8,128)(2,1)S(1)}, bf16[512,256]{1,0:T(8,128)(2,1)S(1)}, u32[]{:S(2)}, u32[]{:S(2)}) collective-permute-start(bf16[512,256]{1,0:T(8,128)(2,1)S(1)} %collective-permute-done.r1_ref), channel_id=1, source_target_pairs={{0,16},{8,24},{16,32},{24,40},{32,48},{40,56},{48,64},{56,72},{64,... | collective-permute-start | bytes 786440 | tf_op jit(solution)/shard_map/ppermute | solution.py:195
  26.9 2.6 %collective-permute-start.3 = (f32[8,512]{1,0:T(8,128)S(1)}, f32[8,512]{1,0:T(8,128)S(1)}, u32[]{:S(2)}, u32[]{:S(2)}) collective-permute-start(f32[8,512]{1,0:T(8,128)S(1)} %bitcast.4), channel_id=1, source_target_pairs={{0,8},{8,0},{16,24},{24,16},{32,40},{40,32},{48,56},{56,48},{64,72... | collective-permute-start | bytes 49160 | tf_op jit(solution)/shard_map/ppermute | solution.py:199
  29.4 10.0 %collective-permute-start.4 = (f32[16,512]{1,0:T(8,128)S(1)}, f32[16,512]{1,0:T(8,128)S(1)}, u32[]{:S(2)}, u32[]{:S(2)}) collective-permute-start(f32[16,512]{1,0:T(8,128)S(1)} %pad_maximum_fusion.ids_ref), channel_id=1, source_target_pairs={{0,16},{8,24},{16,32},{24,40},{32,48},{40,56},{48,64},{56,72},{64,... | collective-permute-start | bytes 98312 | tf_op jit(solution)/shard_map/ppermute | solution.py:195
  33.6 9.5 %collective-permute-start.5 = (f32[16,512]{1,0:T(8,128)S(1)}, f32[16,512]{1,0:T(8,128)S(1)}, u32[]{:S(2)}, u32[]{:S(2)}) collective-permute-start(f32[16,512]{1,0:T(8,128)S(1)} %pad_maximum_fusion.ids_ref), channel_id=1, source_target_pairs={{0,32},{8,40},{16,48},{24,56},{32,64},{40,72},{48,80},{56,88},{64,... | collective-permute-start | bytes 98312 | tf_op jit(solution)/shard_map/ppermute | solution.py:195
  38.7 22.6 %collective-permute-start.2 = (bf16[512,256]{1,0:T(8,128)(2,1)S(1)}, bf16[512,256]{1,0:T(8,128)(2,1)S(1)}, u32[]{:S(2)}, u32[]{:S(2)}) collective-permute-start(bf16[512,256]{1,0:T(8,128)(2,1)S(1)} %collective-permute-done.1.r2_ref), channel_id=1, source_target_pairs={{0,8},{8,0},{16,24},{24,16},{32,40},{40,32},{48,56},{56,48},{64,72... | collective-permute-start | bytes 786440 | tf_op jit(solution)/shard_map/ppermute | solution.py:199

commit v2 on v0

v2 whole, which is shorter than its diff:
```python
import functools

import jax
import jax.numpy as jnp
import numpy as np
from jax import lax
from jax.experimental import pallas as pl
from jax.experimental.pallas import tpu as pltpu
from jax.sharding import PartitionSpec as P

HEAD = 128
GROUP = 8
TOK = 512
N_CTX = 32
THETA = 1000000.0
NEG = -1e30
SCALE = float(np.log2(np.e) / np.sqrt(HEAD))
HALF = TOK // 2
ROWS = GROUP * HALF
KVH = 8
SPARE = 16


def rotary_table():
    half = HEAD // 2
    inv = np.float32(THETA) ** (-(np.float32(2.0) * np.arange(half, dtype=np.float32)) / np.float32(HEAD))
    angle = np.arange(N_CTX * TOK, dtype=np.float32)[:, None] * inv.astype(np.float32)[None, :]
    wide = angle.astype(np.float64)
    cosine, sine = np.cos(wide), np.sin(wide)
    table = np.concatenate([cosine, cosine, -sine, sine], axis=1).astype(np.float32)
    return table.reshape(N_CTX, TOK, 2 * HEAD)


def rotate(x, table):
    x = x.astype(jnp.float32)
    return (x * table[:, :HEAD] + pltpu.roll(x, HEAD // 2, 1) * table[:, HEAD:]).astype(jnp.bfloat16)


def pack_kernel(ctx_ref, ids, k, v, table_hbm, out, table, sem):
    copy = pltpu.make_async_copy(table_hbm.at[ctx_ref[0]], table, sem)
    copy.start()
    out[:TOK, HEAD:] = v[...]
    pieces, size = ids.shape
    wide = jnp.concatenate([ids[...], jnp.zeros((pieces, 2 * HEAD - size), jnp.float32)], axis=1)
    wide = jnp.concatenate([wide, jnp.zeros((SPARE - pieces, 2 * HEAD), jnp.float32)], axis=0)
    out[TOK:] = wide.astype(jnp.bfloat16)
    copy.wait()
    out[:TOK, :HEAD] = rotate(k[...], table)


def twice(x):
    return jnp.concatenate([x, x], axis=-1)


def widened(x, width):
    return jnp.concatenate([x] * (width // HEAD), axis=-1)


def pieces_of(message):
    return message[TOK:].astype(jnp.float32)


def id_row(parts):
    size = TOK // KVH
    parts = parts[:KVH]
    lane = lax.broadcasted_iota(jnp.int32, (2 * HEAD, TOK), 1)
    place = (lax.rem(lane, size) == lax.broadcasted_iota(jnp.int32, (2 * HEAD, TOK), 0)).astype(jnp.float32)
    spread = jnp.dot(parts, place, preferred_element_type=jnp.float32)
    mine = lax.broadcasted_iota(jnp.int32, (KVH, TOK), 1) // size
    mine = mine == lax.broadcasted_iota(jnp.int32, (KVH, TOK), 0)
    return jnp.sum(jnp.where(mine, spread, 0.0), axis=0, keepdims=True)


def matches(block, first):
    return jnp.sum(jnp.where(block == first, 1, 0))


def prepare_block(kv, kt, va):
    kt[...] = kv[:TOK, :HEAD].T
    va[:, :HEAD] = kv[:TOK, HEAD:]
    va[:, HEAD:] = jnp.ones((TOK, HEAD), jnp.bfloat16)


def own_half(half, queries, kt, va, column, row, m, acc):
    width = (half + 1) * HALF
    rows = slice(half * HALF, width)
    key = lax.broadcasted_iota(jnp.int32, (HALF, width), 1)
    query = half * HALF + lax.broadcasted_iota(jnp.int32, (HALF, width), 0)
    same = widened(column[rows], width) == row[:, :width]
    bias = jnp.where(same & (key <= query), 0.0, NEG)
    s = jnp.dot(queries[half], kt[:, :width], preferred_element_type=jnp.float32)
    s = s.reshape(GROUP, HALF, width) * SCALE + bias[None]
    top = jnp.broadcast_to(jnp.max(s, axis=2, keepdims=True), (GROUP, HALF, HEAD))
    p = jnp.exp2(s - widened(top, width)).reshape(ROWS, width).astype(jnp.bfloat16)
    m[half] = top.reshape(ROWS, HEAD)
    acc[half] = jnp.dot(p, va[:width], preferred_element_type=jnp.float32)


def far_half(half, queries, kt, va, base, start, count, m, acc):
    kpos = base + lax.broadcasted_iota(jnp.int32, (1, TOK), 1)
    key_bias = jnp.where(kpos >= start, 0.0, NEG)
    live = half * HALF + lax.broadcasted_iota(jnp.int32, (HALF, HEAD), 0) < count
    s = jnp.dot(queries[half], kt[...], preferred_element_type=jnp.float32)
    s = (s * SCALE + key_bias).reshape(GROUP, HALF, TOK)
    old = m[half].reshape(GROUP, HALF, HEAD)
    top = jnp.where(live[None], jnp.max(s, axis=2, keepdims=True), NEG)
    new = jnp.maximum(old, top)
    shift = jnp.where(live[None], new, -NEG)
    p = jnp.exp2(s - widened(shift, TOK)).reshape(ROWS, TOK).astype(jnp.bfloat16)
    factor = jnp.exp2(old - new).reshape(ROWS, HEAD)
    m[half] = new.reshape(ROWS, HEAD)
    update = jnp.dot(p, va[...], preferred_element_type=jnp.float32)
    acc[half] = acc[half] * twice(factor) + update


def far_blocks(bases, messages, ctx_base, queries, kt, va, start, count, m, acc):
    def seen(base):
        return (base < ctx_base) & (base + TOK > start)

    for slot, (base, message) in enumerate(zip(bases, messages)):

        @pl.when(seen(base))
        def _():
            prepare_block(message, kt.at[slot], va.at[slot])

    def visit(slot, carry):
        base = bases[0]
        for i in range(1, len(bases)):
            base = jnp.where(slot == i, bases[i], base)

        @pl.when(seen(base))
        def _():
            def body(half, inner):
                far_half(half, queries, kt.at[slot], va.at[slot], base, start, count, m, acc)
                return inner

            lax.fori_loop(0, (count + HALF - 1) // HALF, body, 0)

        return carry

    lax.fori_loop(0, len(bases), visit, 0)


def finish(acc, out):
    for half in range(2):
        for h in range(GROUP):
            a = acc[half, h * HALF : (h + 1) * HALF]
            out[half * HALF : (half + 1) * HALF, h * HEAD : (h + 1) * HEAD] = (
                a[:, :HEAD] / a[:, HEAD:]
            ).astype(jnp.bfloat16)


def own_kernel(ctx_ref, own, table_hbm, q_hbm, queries, m, acc, table, raw, kt, va, sems):
    copies = [
        pltpu.make_async_copy(table_hbm.at[ctx_ref[0]], table, sems.at[0]),
        pltpu.make_async_copy(q_hbm, raw, sems.at[1]),
    ]
    for copy in copies:
        copy.start()
    row = id_row(pieces_of(own))
    column = jnp.broadcast_to(row, (HEAD, TOK)).T
    prepare_block(own, kt, va)
    for copy in copies:
        copy.wait()
    for h in range(GROUP):
        turned = rotate(raw[:, h * HEAD : (h + 1) * HEAD], table)
        for half in range(2):
            queries[half, h * HALF : (h + 1) * HALF] = turned[half * HALF : (half + 1) * HALF]
    for half in range(2):
        own_half(half, queries, kt, va, column, row, m, acc)


def near_start(ctx, own, sib, r1, r1s):
    mine = pieces_of(own)
    first = mine[:1, :1]
    before = matches(pieces_of(sib), first) * lax.rem(ctx, 2)
    before = before + matches(pieces_of(r1), first) + matches(pieces_of(r1s), first)
    return ctx * TOK - before, matches(mine, first), first


def chip_before(ctx):
    return (ctx - 2 - lax.rem(ctx, 2)) * TOK


def near_kernel(ctx_ref, own, sib, r1, r1s, queries, m_in, acc_in, out_hbm, m, acc, kt, va, out, sem):
    ctx = ctx_ref[0]
    other = ctx + 1 - 2 * lax.rem(ctx, 2)
    start, count, _ = near_start(ctx, own, sib, r1, r1s)
    bases = [other * TOK, (ctx - 2) * TOK, (other - 2) * TOK]
    far_blocks(bases, [sib, r1, r1s], ctx * TOK, queries, kt, va, start, count, m, acc)
    finish(acc, out)
    send = pltpu.make_async_copy(out, out_hbm, sem)
    send.start()
    send.wait()


def last_kernel(
    ctx_ref, own, sib, r1, r1s, r2, r2s, queries, m_in, acc_in, done_hbm,
    out_hbm, m, acc, kt, va, out, sem,
):
    ctx = ctx_ref[0]
    other = ctx + 1 - 2 * lax.rem(ctx, 2)
    near, count, first = near_start(ctx, own, sib, r1, r1s)

    @pl.when((near <= chip_before(ctx)) & (ctx >= 4))
    def _():
        start = near - matches(pieces_of(r2), first) - matches(pieces_of(r2s), first)

        @pl.when(start < near)
        def _():
            bases = [(ctx - 4) * TOK, (other - 4) * TOK]
            far_blocks(bases, [r2, r2s], ctx * TOK, queries, kt, va, start, count, m, acc)
            finish(acc, out)
            send = pltpu.make_async_copy(out, out_hbm, sem)
            send.start()
            send.wait()


IN_SMEM = pl.BlockSpec(memory_space=pltpu.SMEM)
IN_VMEM = pl.BlockSpec(memory_space=pltpu.VMEM)
IN_HBM = pl.BlockSpec(memory_space=pltpu.HBM)
MESSAGE = jax.ShapeDtypeStruct((TOK + SPARE, 2 * HEAD), jnp.bfloat16)
OUT = jax.ShapeDtypeStruct((TOK, GROUP * HEAD), jnp.bfloat16)
QUERIES = jax.ShapeDtypeStruct((2, ROWS, HEAD), jnp.bfloat16)
TOP = jax.ShapeDtypeStruct((2, ROWS, HEAD), jnp.float32)
ACC = jax.ShapeDtypeStruct((2, ROWS, 2 * HEAD), jnp.float32)
TABLE = pltpu.VMEM((TOK, 2 * HEAD), jnp.float32)
LIMIT = 44 * 2**20


def like(t):
    return pltpu.VMEM(t.shape, t.dtype)


def blocks(count):
    lead = (count,) if count else ()
    return [pltpu.VMEM(lead + (HEAD, TOK), jnp.bfloat16), pltpu.VMEM(lead + (TOK, 2 * HEAD), jnp.bfloat16)]


def call(kernel, name, ins, outs, scratch, flops, **more):
    specs, types = zip(*outs)
    return pl.pallas_call(
        kernel,
        in_specs=[IN_SMEM] + ins,
        out_specs=list(specs),
        out_shape=list(types),
        scratch_shapes=scratch,
        compiler_params=pltpu.CompilerParams(vmem_limit_bytes=LIMIT),
        cost_estimate=pl.CostEstimate(flops=flops, bytes_accessed=2**21, transcendentals=0),
        name=name,
        **more,
    )


def shifted(value, steps):
    return lax.ppermute(value, "ctx", [(i, i + steps) for i in range(N_CTX - steps)])


def swapped(value):
    return lax.ppermute(value, "ctx", [(i, i ^ 1) for i in range(N_CTX)])


def local(q_proj, key_projection, value_projection, doc_ids):
    table = jnp.asarray(rotary_table())
    ctx = lax.axis_index("ctx").astype(jnp.int32).reshape(1)
    mine = jnp.broadcast_to((doc_ids + 1).astype(jnp.float32), (KVH, doc_ids.shape[0]))
    ids = lax.all_to_all(mine, "kvh", 0, 0, tiled=True)
    dma = pltpu.SemaphoreType.DMA
    (own,) = call(
        pack_kernel, "pack", [IN_VMEM] * 3 + [IN_HBM], [(IN_VMEM, MESSAGE)], [TABLE, dma], 10**6
    )(ctx, ids, key_projection, value_projection, table)
    r1 = shifted(own, 2)
    sib = swapped(own)
    queries, m, acc = call(
        own_kernel,
        "own",
        [IN_VMEM] + [IN_HBM] * 2,
        [(IN_VMEM, QUERIES), (IN_VMEM, TOP), (IN_VMEM, ACC)],
        [TABLE, like(OUT)] + blocks(0) + [dma((2,))],
        3 * 10**9,
    )(ctx, own, table, q_proj)
    r1, queries = lax.optimization_barrier((r1, queries))
    r2 = shifted(r1, 2)
    r1s = swapped(r1)
    out, m, acc = call(
        near_kernel,
        "near",
        [IN_VMEM] * 7,
        [(IN_HBM, OUT), (IN_VMEM, TOP), (IN_VMEM, ACC)],
        blocks(3) + [like(OUT), dma],
        8 * 10**9,
        input_output_aliases={6: 1, 7: 2},
    )(ctx, own, sib, r1, r1s, queries, m, acc)
    r2, m = lax.optimization_barrier((r2, m))
    r2s = swapped(r2)
    out, _, _ = call(
        last_kernel,
        "last",
        [IN_VMEM] * 9 + [IN_HBM],
        [(IN_HBM, OUT), (IN_VMEM, TOP), (IN_VMEM, ACC)],
        blocks(2) + [like(OUT), dma],
        10**9,
        input_output_aliases={8: 1, 9: 2, 10: 0},
    )(ctx, own, sib, r1, r1s, r2, r2s, queries, m, acc, out)
    return out


def solution(mesh):
    in_specs = (P("ctx", "kvh"), P("ctx", "kvh"), P("ctx", "kvh"), P(("ctx", "kvh")))
    return jax.shard_map(
        local, mesh=mesh, in_specs=in_specs, out_specs=P("ctx", "kvh"), check_vma=False
    )
```

time: 128 us -> 48.3 us (0.38)
  the two profiles are of different devices: /device:TPU:16 before, /device:TPU:128 now
where the time goes in v2:
time: 48.3 us; the launch traced here: 48.2 us
  Pallas kernels  23.8 us (49%)
  waiting for transfers between devices  11 us (23%)
  starting transfers between devices  10.2 us (21%)
  local copies, waits for them, and re-layouts  2.41 us (5%)
  other arithmetic  0.66 us (1%)
    pallas_call x1, Pallas kernels, local(): call(last_kernel, 'last', [IN_VMEM] * 9 + [IN_HBM], [(IN_HBM, OUT), (IN_V...  9.07 us
    pallas_call x1, Pallas kernels, local(): call(near_kernel, 'near', [IN_VMEM] * 7, [(IN_HBM, OUT), (IN_VMEM, TOP),...  8.96 us
    all_to_all x1, waiting for transfers between devices, local(): ids = lax.all_to_all(mine, 'kvh', 0, 0, tiled=True)  6.08 us
    all_to_all x1, starting transfers between devices, local(): ids = lax.all_to_all(mine, 'kvh', 0, 0, tiled=True)  5.31 us
    ppermute x2, starting transfers between devices, shifted(): lax.ppermute(value, 'ctx', [(i, i + steps) for i in range(N_CTX - steps)])  4.84 us
    pallas_call x1, Pallas kernels, local(): call(own_kernel, 'own', [IN_VMEM] + [IN_HBM] * 2, [(IN_VMEM, QUERIES), (I...  4.52 us
    ppermute x2, waiting for transfers between devices, shifted(): lax.ppermute(value, 'ctx', [(i, i + steps) for i in range(N_CTX - steps)])  3.4 us
    unnamed x6, local copies, waits for them, and re-layouts  1.81 us
  transfers between devices with their start and end apart: 6, of which 4 were waited for; matrix products, arithmetic and copies ran while one was open for 0% of the time, Pallas kernels for 28%

profile of v2, /device:TPU:128, one launch (start us, length us, event | category | flops | bytes accessed | tf_op | source)
XLA Modules:
  0.0 48.2 jit_solution(14813408749479208143)
XLA Ops:
  0.0 0.7 %add_convert_fusion = f32[64]{0:T(128)S(1)} fusion(s32[64]{0:T(128)} %param.8), kind=kLoop, calls=%fused_computation | loop fusion | flops 128 | bytes 512 | tf_op jit(solution)/shard_map/convert_element_type | solution.py:266
  0.7 0.6 %broadcast_in_dim.3 = f32[8,1,64]{2,1,0:T(1,128)} broadcast(f32[64]{0:T(128)S(1)} %add_convert_fusion), dimensions={2} | broadcast | bytes 2304 | tf_op jit(solution)/shard_map/broadcast_in_dim | solution.py:266
  1.3 5.3 %all-to-all-start = ((f32[8,1,64]{2,1,0:T(1,128)}), f32[8,1,64]{2,1,0:T(1,128)S(1)}, u32[]{:S(2)}, u32[]{:S(2)}) async-start(f32[8,1,64]{2,1,0:T(1,128)} %broadcast_in_dim.3), calls=%async_computation | async-start | bytes 8192 | tf_op jit(solution)/shard_map/all_to_all | solution.py:267
  6.6 6.1 %all-to-all-done = f32[8,1,64]{2,1,0:T(1,128)S(1)} async-done(((f32[8,1,64]{2,1,0:T(1,128)}), f32[8,1,64]{2,1,0:T(1,128)S(1)}, u32[]{:S(2)}, u32[]{:S(2)}) %all-to-all-start) | async-done | bytes 2080 | tf_op jit(solution)/shard_map/all_to_all | solution.py:267
  12.6 0.0 copy-start.1
  12.7 0.9 %copy-done.1 = bf16[512,128]{1,0:T(8,128)(2,1)S(1)} copy-done((bf16[512,128]{1,0:T(8,128)(2,1)S(1)}, bf16[512,128]{1,0:T(8,128)(2,1)}, u32[]{:S(2)}) %copy-start.1) | copy-done | bytes 131096
  13.6 0.0 copy-start.2
  13.6 0.9 %copy-done.2 = bf16[512,128]{1,0:T(8,128)(2,1)S(1)} copy-done((bf16[512,128]{1,0:T(8,128)(2,1)S(1)}, bf16[512,128]{1,0:T(8,128)(2,1)}, u32[]{:S(2)}) %copy-start.2) | copy-done | bytes 131096
  14.5 0.0 copy-start
  14.5 1.2 %pack.1.own = bf16[528,256]{1,0:T(8,128)(2,1)S(1)} custom-call(s32[1]{0:T(128)} %bitcast.ctx_ref, f32[8,64]{1,0:T(8,128)S(1)} %bitcast.2, bf16[512,128]{1,0:T(8,128)(2,1)S(1)} %copy-done.1, bf16[512,128]{1,0:T(8,128)(2,1)S(1)} %copy-done.2, f32[32,512,256]{2,1,0:T(8,128)} %constant.10.clone.table_hbm), custom_call_target="tpu_custom_call" | custom-call | flops 1000000 | bytes 2097152 | tf_op jit(solution)/shard_map/pack/pallas_call | solution.py:269
  15.7 2.9 %collective-permute-start.1 = (bf16[528,256]{1,0:T(8,128)(2,1)S(1)}, bf16[528,256]{1,0:T(8,128)(2,1)S(1)}, u32[]{:S(2)}, u32[]{:S(2)}) collective-permute-start(bf16[528,256]{1,0:T(8,128)(2,1)S(1)} %pack.1.own), channel_id=1, source_target_pairs={{0,16},{8,24},{16,32},{24,40},{32,48},{40,56},{48,64},{56,72},{64,... | collective-permute-start | bytes 811016 | tf_op jit(solution)/shard_map/ppermute | solution.py:256
  18.7 0.1 collective-permute-start
  18.8 0.0 copy-done
  18.8 4.5 %own.1 = (bf16[2,2048,128]{2,1,0:T(8,128)(2,1)S(1)}, f32[2,2048,128]{2,1,0:T(8,128)S(1)}, f32[2,2048,256]{2,1,0:T(8,128)S(1)}) custom-call(s32[1]{0:T(128)} %bitcast.ctx_ref, bf16[528,256]{1,0:T(8,128)(2,1)S(1)} %pack.1.own, f32[32,512,256]{2,1,0:T(8,128)} %constant.10.clone.table_hbm, bf16[512,1024]{1,0:T(8,128)(2,1)S(1)} %copy-done), custom_call_target="tpu_custom_call" | custom-call | flops 3000000000 | bytes 2097152 | tf_op jit(solution)/shard_map/own/pallas_call | solution.py:274
  23.3 2.3 %collective-permute-done.1.r1 = bf16[528,256]{1,0:T(8,128)(2,1)S(1)} collective-permute-done((bf16[528,256]{1,0:T(8,128)(2,1)S(1)}, bf16[528,256]{1,0:T(8,128)(2,1)S(1)}, u32[]{:S(2)}, u32[]{:S(2)}) %collective-permute-start.1) | collective-permute-done | bytes 270368 | tf_op jit(solution)/shard_map/ppermute | solution.py:256
  25.6 0.0 collective-permute-start.2
  25.6 1.9 %collective-permute-start.3 = (bf16[528,256]{1,0:T(8,128)(2,1)S(1)}, bf16[528,256]{1,0:T(8,128)(2,1)S(1)}, u32[]{:S(2)}, u32[]{:S(2)}) collective-permute-start(bf16[528,256]{1,0:T(8,128)(2,1)S(1)} %collective-permute-done.1.r1), channel_id=1, source_target_pairs={{0,16},{8,24},{16,32},{24,40},{32,48},{40,56},{48,64},{56,72},{64,... | collective-permute-start | bytes 811016 | tf_op jit(solution)/shard_map/ppermute | solution.py:256
  27.5 0.0 collective-permute-done.sib
  27.5 0.0 collective-permute-done.2.r1s
  27.6 9.0 %near.1 = (bf16[512,1024]{1,0:T(8,128)(2,1)}, f32[2,2048,128]{2,1,0:T(8,128)S(1)}, f32[2,2048,256]{2,1,0:T(8,128)S(1)}) custom-call(s32[1]{0:T(128)} %bitcast.ctx_ref, bf16[528,256]{1,0:T(8,128)(2,1)S(1)} %pack.1.own, bf16[528,256]{1,0:T(8,128)(2,1)S(1)} %collective-permute-done.sib, ...), custom_call_target="tpu_custom_call", output_to_operand_aliasing={{1}: (6, {}), {2}: (7, {})} | custom-call | flops 8000000000 | bytes 2097152 | tf_op jit(solution)/shard_map/near/pallas_call | solution.py:285
  36.5 1.1 %collective-permute-done.3.r2 = bf16[528,256]{1,0:T(8,128)(2,1)S(1)} collective-permute-done((bf16[528,256]{1,0:T(8,128)(2,1)S(1)}, bf16[528,256]{1,0:T(8,128)(2,1)S(1)}, u32[]{:S(2)}, u32[]{:S(2)}) %collective-permute-start.3) | collective-permute-done | bytes 270368 | tf_op jit(solution)/shard_map/ppermute | solution.py:256
  37.6 0.0 collective-permute-start.4
  37.6 1.5 %collective-permute-done.4.r2s = bf16[528,256]{1,0:T(8,128)(2,1)S(1)} collective-permute-done((bf16[528,256]{1,0:T(8,128)(2,1)S(1)}, bf16[528,256]{1,0:T(8,128)(2,1)S(1)}, u32[]{:S(2)}, u32[]{:S(2)}) %collective-permute-start.4) | collective-permute-done | bytes 270368 | tf_op jit(solution)/shard_map/ppermute | solution.py:260
  39.2 9.1 %last.1 = (bf16[512,1024]{1,0:T(8,128)(2,1)}, f32[2,2048,128]{2,1,0:T(8,128)S(1)}, f32[2,2048,256]{2,1,0:T(8,128)S(1)}) custom-call(s32[1]{0:T(128)} %bitcast.ctx_ref, bf16[528,256]{1,0:T(8,128)(2,1)S(1)} %pack.1.own, bf16[528,256]{1,0:T(8,128)(2,1)S(1)} %collective-permute-done.sib, ...), custom_call_target="tpu_custom_call", output_to_operand_aliasing={{1}: (8, {}), {2}: (9, {}), {0}: (10, {})} | custom-call | flops 1000000000 | bytes 2097152 | tf_op jit(solution)/shard_map/last/pallas_call | solution.py:296
Async XLA Ops:
  1.3 11.4 %all-to-all-start = ((f32[8,1,64]{2,1,0:T(1,128)}), f32[8,1,64]{2,1,0:T(1,128)S(1)}, u32[]{:S(2)}, u32[]{:S(2)}) async-start(f32[8,1,64]{2,1,0:T(1,128)} %broadcast_in_dim.3), calls=%async_computation | async-start | bytes 8192 | tf_op jit(solution)/shard_map/all_to_all | solution.py:267
  12.6 0.9 %copy-start.1 = (bf16[512,128]{1,0:T(8,128)(2,1)S(1)}, bf16[512,128]{1,0:T(8,128)(2,1)}, u32[]{:S(2)}) copy-start(bf16[512,128]{1,0:T(8,128)(2,1)} %k.1) | copy-start | bytes 393220
  13.6 0.9 %copy-start.2 = (bf16[512,128]{1,0:T(8,128)(2,1)S(1)}, bf16[512,128]{1,0:T(8,128)(2,1)}, u32[]{:S(2)}) copy-start(bf16[512,128]{1,0:T(8,128)(2,1)} %v.1) | copy-start | bytes 393220
  14.5 4.3 %copy-start = (bf16[512,1024]{1,0:T(8,128)(2,1)S(1)}, bf16[512,1024]{1,0:T(8,128)(2,1)}, u32[]{:S(2)}) copy-start(bf16[512,1024]{1,0:T(8,128)(2,1)} %q_hbm.1) | copy-start | bytes 3145732
  15.7 9.9 %collective-permute-start.1 = (bf16[528,256]{1,0:T(8,128)(2,1)S(1)}, bf16[528,256]{1,0:T(8,128)(2,1)S(1)}, u32[]{:S(2)}, u32[]{:S(2)}) collective-permute-start(bf16[528,256]{1,0:T(8,128)(2,1)S(1)} %pack.1.own), channel_id=1, source_target_pairs={{0,16},{8,24},{16,32},{24,40},{32,48},{40,56},{48,64},{56,72},{64,... | collective-permute-start | bytes 811016 | tf_op jit(solution)/shard_map/ppermute | solution.py:256
  18.7 8.9 %collective-permute-start = (bf16[528,256]{1,0:T(8,128)(2,1)S(1)}, bf16[528,256]{1,0:T(8,128)(2,1)S(1)}, u32[]{:S(2)}, u32[]{:S(2)}) collective-permute-start(bf16[528,256]{1,0:T(8,128)(2,1)S(1)} %pack.1.own), channel_id=1, source_target_pairs={{0,8},{8,0},{16,24},{24,16},{32,40},{40,32},{48,56},{56,48},{64,72... | collective-permute-start | bytes 811016 | tf_op jit(solution)/shard_map/ppermute | solution.py:260
  25.6 1.9 %collective-permute-start.2 = (bf16[528,256]{1,0:T(8,128)(2,1)S(1)}, bf16[528,256]{1,0:T(8,128)(2,1)S(1)}, u32[]{:S(2)}, u32[]{:S(2)}) collective-permute-start(bf16[528,256]{1,0:T(8,128)(2,1)S(1)} %collective-permute-done.1.r1), channel_id=1, source_target_pairs={{0,8},{8,0},{16,24},{24,16},{32,40},{40,32},{48,56},{56,48},{64,72... | collective-permute-start | bytes 811016 | tf_op jit(solution)/shard_map/ppermute | solution.py:260
  25.6 12.0 %collective-permute-start.3 = (bf16[528,256]{1,0:T(8,128)(2,1)S(1)}, bf16[528,256]{1,0:T(8,128)(2,1)S(1)}, u32[]{:S(2)}, u32[]{:S(2)}) collective-permute-start(bf16[528,256]{1,0:T(8,128)(2,1)S(1)} %collective-permute-done.1.r1), channel_id=1, source_target_pairs={{0,16},{8,24},{16,32},{24,40},{32,48},{40,56},{48,64},{56,72},{64,... | collective-permute-start | bytes 811016 | tf_op jit(solution)/shard_map/ppermute | solution.py:256
  37.6 1.5 %collective-permute-start.4 = (bf16[528,256]{1,0:T(8,128)(2,1)S(1)}, bf16[528,256]{1,0:T(8,128)(2,1)S(1)}, u32[]{:S(2)}, u32[]{:S(2)}) collective-permute-start(bf16[528,256]{1,0:T(8,128)(2,1)S(1)} %collective-permute-done.3.r2), channel_id=1, source_target_pairs={{0,8},{8,0},{16,24},{24,16},{32,40},{40,32},{48,56},{56,48},{64,72... | collective-permute-start | bytes 811016 | tf_op jit(solution)/shard_map/ppermute | solution.py:260
